TPU v7x, 32 devices: a whole 2x2x4 slice. The times are simulated.
32 devices in a mesh: row: 4 (over y, x), col: 8 (over z, core).
Axes of the slice: x: 2, y: 2, z: 4, core: 2. Of those that a mesh axis runs over, the one named last changes fastest.
Arguments:
- hidden: bfloat16 [640, 7168], P('col', 'row'), may hold values from -6 to 6
- ln_gain: bfloat16 [7168], P('row'), may hold values from 0.099609375 to 1.8984375
- ln_shift: bfloat16 [7168], P('row'), may hold values from -3 to 3
- qkv_weight: bfloat16 [7168, 12288], P('row', 'col'), may hold values from -0.0625 to 0.0625
- qkv_bias: bfloat16 [12288], P('col'), may hold values from -5.351432 to 5.351432
- out_weight: bfloat16 [4096, 7168], P('row', 'col'), may hold values from -0.09375 to 0.09375
- out_bias: bfloat16 [7168], P('col'), may hold values from -3 to 3
- down_qkv: bfloat16 [64, 7168, 16], P(None, 'row'), may hold values from -0.0625 to 0.0625
- up_qkv: bfloat16 [64, 16, 12288], P(None, None, 'col'), may hold values from -1.5 to 1.5
- down_out: bfloat16 [64, 16, 4096], P(None, None, 'col'), may hold values from -0.09375 to 0.09375
- up_out: bfloat16 [64, 16, 7168], P(None, None, 'col'), may hold values from -1.5 to 1.5
- prompt_lens: int32 [4], replicated, may hold values from 1 to 80, as said below
- suffix_lens: int32 [4, 16], replicated, may hold values from 1 to 5, as said below
- group_sizes: int32 [4], replicated, may hold values from 8 to 16, as said below
- group_adapter_choice: int32 [4], replicated, may hold values from 0 to 15
- chosen: int32 [16], replicated, may hold values from 0 to 63, as said below
Outputs:
- attn_out: bfloat16 [640, 7168], P('row', 'col')
Inputs may be any that keep to these rules, and one draw needn't show every extreme that they name: `prompt_lens`: one group, drawn from the seed, has a prompt of exactly 80 tokens, 16 requests and every suffix 5 long, so it fills all 160 slots. `suffix_lens`: entries past a group's number of requests are not used. `group_sizes`: A group's prompt and its live suffixes take at most 160 slots. `chosen`: 16 different bank indices.
All inputs are finite; a program needn't handle non-finite values.
Results may differ from a plain program's by a relative error of at most 0.012.
The roundings to bfloat16 on the way count: a program that leaves them out, or rounds other values in their place, can miss the bound.
Values may be sent and summed in bfloat16 or wider, within the bound.
A program may use at most 128 MiB of HBM per device.

v0:
```python
import jax
import jax.numpy as jnp
from jax import lax
from jax.sharding import PartitionSpec as P

HEAD_SIZE = 128
GCAP = 160
WIN = 53


def broadcast(x, axis, root):
    mine = lax.axis_index(axis) == root
    return lax.psum(jnp.where(mine, x, jnp.zeros_like(x)), axis)


def group_layout(prompt, count, suffix):
    offsets = jnp.arange(GCAP, dtype=jnp.int32)
    chosen_adapter_index = jnp.arange(suffix.shape[0], dtype=jnp.int32)
    live_lens = jnp.where(chosen_adapter_index < count, suffix, 0)
    end_at = prompt + jnp.cumsum(live_lens)
    group_start_rows = end_at - live_lens
    request = jnp.sum((offsets[:, None] >= end_at[None, :]).astype(jnp.int32), axis=1)
    in_prompt = offsets < prompt
    live_rows = in_prompt | (request < count)
    group_begin_row = jnp.sum(
        jnp.where(chosen_adapter_index[None, :] == request[:, None], group_start_rows[None, :], 0),
        axis=1,
    )
    position = jnp.where(in_prompt, offsets, prompt + offsets - group_begin_row)
    request_of = jnp.where(in_prompt, -1, request)
    return (live_rows, request_of, position)


def key_mask(live_rows, request_of, position):
    shared = (request_of[None, :] == -1) | (request_of[None, :] == request_of[:, None])
    causal = position[None, :] <= position[:, None]
    within = (position[:, None] - position[None, :] < WIN) | (position[None, :] == 0)
    allowed = live_rows[:, None] & live_rows[None, :] & shared & causal & within
    first_key = jnp.arange(GCAP)[None, :] == 0
    return jnp.where(live_rows[:, None], allowed, first_key)


def attention(queries, key_rows, value_rows, allowed):
    scores = jnp.einsum("qhe,khe->hqk", queries, key_rows, preferred_element_type=jnp.float32)
    scores = jnp.where(allowed[None], scores, -1e30)
    highest = jnp.max(scores, axis=2, keepdims=True)
    weights = jnp.where(allowed[None], jnp.exp(scores - highest), 0.0)
    probs = (weights / jnp.sum(weights, axis=2, keepdims=True)).astype(jnp.bfloat16)
    mixed_rows = jnp.einsum("hqk,khe->qhe", probs, value_rows, preferred_element_type=jnp.float32)
    return mixed_rows.astype(jnp.bfloat16).reshape(queries.shape[0], -1)


def local(
    hidden,
    ln_gain,
    ln_shift,
    qkv_weight,
    qkv_bias,
    out_weight,
    out_bias,
    down_qkv,
    up_qkv,
    down_out,
    up_out,
    prompt_lens,
    suffix_lens,
    group_sizes,
    group_adapter_choice,
    chosen,
):
    row_index = lax.axis_index("row")
    row_count = lax.axis_size("row")
    adapters = chosen[group_adapter_choice]
    own_adapter = adapters[row_index]
    low_rank = down_qkv.shape[2]
    features, gain_full, shift_full = (
        lax.all_gather(hidden, "row", axis=1, tiled=True),
        lax.all_gather(ln_gain, "row", axis=0, tiled=True),
        lax.all_gather(ln_shift, "row", axis=0, tiled=True),
    )
    widened = features.astype(jnp.float32)
    average = jnp.mean(widened, axis=1, keepdims=True)
    centred = widened - average
    spread = jnp.mean(centred * centred, axis=1, keepdims=True)
    normed = (
        centred * lax.rsqrt(spread + 1e-05) * gain_full.astype(jnp.float32)
        + shift_full.astype(jnp.float32)
    ).astype(jnp.bfloat16)
    per_group = lax.axis_size("col") // row_count
    received = []
    for offset in range(per_group):
        received.append(broadcast(normed, "col", row_index * per_group + offset))
    group_rows = jnp.concatenate(received, axis=0)
    lowered = jnp.transpose(down_qkv[adapters], (1, 0, 2)).reshape(
        down_qkv.shape[1], row_count * low_rank
    )
    sliced = group_rows
    own_down = lax.dynamic_slice_in_dim(
        lax.all_gather(lowered, "row", axis=0, tiled=True), row_index * low_rank, low_rank, 1
    )
    projected = jnp.dot(
        sliced,
        lax.all_gather(qkv_weight, "row", axis=0, tiled=True),
        preferred_element_type=jnp.float32,
    )
    reduced = jnp.dot(sliced, own_down, preferred_element_type=jnp.float32)
    projected = (
        projected
        + qkv_bias.astype(jnp.float32)
        + jnp.dot(
            reduced.astype(jnp.bfloat16), up_qkv[own_adapter], preferred_element_type=jnp.float32
        )
    )
    heads_here = projected.shape[1] // (3 * HEAD_SIZE)
    shaped = projected.reshape(GCAP, heads_here, 3, HEAD_SIZE)
    queries = (shaped[:, :, 0] * HEAD_SIZE ** (-0.5)).astype(jnp.bfloat16)
    key_rows = shaped[:, :, 1].astype(jnp.bfloat16)
    value_rows = shaped[:, :, 2].astype(jnp.bfloat16)
    live_rows, request_of, position = group_layout(
        prompt_lens[row_index], group_sizes[row_index], suffix_lens[row_index]
    )
    mixed_rows = attention(queries, key_rows, value_rows, key_mask(live_rows, request_of, position))
    down_here = down_out[own_adapter]
    all_heads, down_full = (
        lax.all_gather(mixed_rows, "col", axis=1, tiled=True),
        lax.all_gather(down_here, "col", axis=1, tiled=True),
    )
    reduced_out = lax.dot_general(
        all_heads, down_full, (((1,), (1,)), ((), ())), preferred_element_type=jnp.float32
    ).astype(jnp.bfloat16)
    sliced = all_heads
    combined = jnp.dot(
        sliced,
        lax.all_gather(out_weight, "row", axis=0, tiled=True),
        preferred_element_type=jnp.float32,
    )
    result = (
        combined
        + out_bias.astype(jnp.float32)
        + jnp.dot(reduced_out, up_out[own_adapter], preferred_element_type=jnp.float32)
    )
    return (result * live_rows[:, None].astype(jnp.float32)).astype(jnp.bfloat16)


def solution(mesh):
    in_specs = (
        P("col", "row"),
        P("row"),
        P("row"),
        P("row", "col"),
        P("col"),
        P("row", "col"),
        P("col"),
        P(None, "row", None),
        P(None, None, "col"),
        P(None, None, "col"),
        P(None, None, "col"),
        P(),
        P(),
        P(),
        P(),
        P(),
    )
    out_specs = P("row", "col")
    return jax.shard_map(local, mesh=mesh, in_specs=in_specs, out_specs=out_specs, check_vma=False)
```

profile of v0, /device:TPU:0, one launch (start us, length us, event | category | flops | bytes accessed | tf_op | source)
XLA Modules:
  0.0 435.7 jit_solution(17522296022612509488)
XLA Ops:
  6.5 0.7 all-gather.8.cloned.1.call-update
  7.3 0.0 all-reduce.3.cloned.1.call-start
  7.3 0.9 reshape.348
  8.2 9.6 %all-gather.1 = bf16[4,1,1792]{2,1,0:T(2,128)(2,1)S(1)} all-gather(bf16[1,1,1792]{2,1,0:T(2,128)(2,1)S(1)} %reshape.348), channel_id=1, replica_groups=mesh['row'=4,'col'=8] {'row'}, dimensions={0}, use_global_device_ids=true | all-gather | bytes 17920 | tf_op jit(solution)/shard_map/all_gather | solution.py:78
  17.8 0.7 reshape.350
  18.5 8.2 %all-gather.2 = bf16[4,1,1792]{2,1,0:T(2,128)(2,1)S(1)} all-gather(bf16[1,1,1792]{2,1,0:T(2,128)(2,1)S(1)} %reshape.350), channel_id=1, replica_groups=mesh['row'=4,'col'=8] {'row'}, dimensions={0}, use_global_device_ids=true | all-gather | bytes 17920 | tf_op jit(solution)/shard_map/all_gather | solution.py:79
  26.7 12.8 %all-gather.8.cloned.1.call-done = bf16[80,7168]{1,0:T(8,128)(2,1)} async-done(((bf16[80,1792]{1,0:T(8,128)(2,1)}), bf16[80,7168]{1,0:T(8,128)(2,1)}) %all-gather.8.cloned.1.call-update) | async-done | bytes 1146896 | tf_op jit(solution)/shard_map/all_gather | solution.py:77
  39.5 1.6 convert_reduce_fusion
  41.1 1.7 fusion.3
  42.9 2.1 broadcast_select_fusion
  45.1 0.0 all-gather.10.cloned.1.call-start
  45.1 0.7 all-gather.10.cloned.1.call-update
  45.8 0.0 all-gather.14.cloned.1.call-start
  45.9 0.5 all-gather.14.cloned.1.call-update
  46.4 0.0 all-gather.12.cloned.1.call-start
  46.5 0.6 gather_fusion
  47.1 0.6 dynamic_slice.25
  49.0 0.6 dynamic_slice.28
  49.6 0.7 compare_select_fusion.3
  50.3 0.1 copy.32
  50.4 0.6 dynamic_slice.27
  51.7 2.6 gather_fusion.1
  54.3 0.7 add_reduce_fusion
  55.0 0.1 convert_reduce_fusion.1
  55.1 0.7 fusion.36
  55.8 0.1 select_reduce_fusion
  55.9 14.1 %all_gather.28 = bf16[7168,64]{0,1:T(8,128)(2,1)} all-gather(bf16[1792,64]{0,1:T(8,128)(2,1)S(1)} %bitcast.63), channel_id=1, replica_groups=mesh['row'=4,'col'=8] {'row'}, dimensions={0}, use_global_device_ids=true | all-gather | bytes 1146880 | tf_op jit(solution)/shard_map/all_gather | solution.py:99
  69.9 0.6 broadcast_compare_fusion
  70.6 1.3 fusion.44
  71.8 0.2 fusion.21
  72.0 39.9 %all-reduce.3.cloned.1.call-done = (bf16[80,7168]{1,0:T(8,128)(2,1)}, bf16[80,7168]{1,0:T(8,128)(2,1)}) async-done(((bf16[80,7168]{1,0:T(8,128)(2,1)}, bf16[80,7168]{1,0:T(8,128)(2,1)}), (bf16[80,7168]{1,0:T(8,128)(2,1)}, bf16[80,7168]{1,0:T(8,128)(2,1)})) %all-reduce.3.cloned.1.call-update) | async-done | bytes 2293776 | tf_op jit(solution)/shard_map/psum | solution.py:13
  111.9 2.5 constant_dynamic-update-slice_fusion.1
  114.4 1.1 constant_dynamic-update-slice_fusion
  115.5 199.2 %all-gather.10.cloned.1.call-done = bf16[7168,1536]{1,0:T(8,128)(2,1)} async-done(((bf16[1792,1536]{1,0:T(8,128)(2,1)}), bf16[7168,1536]{1,0:T(8,128)(2,1)}) %all-gather.10.cloned.1.call-update) | async-done | bytes 22020112 | tf_op jit(solution)/shard_map/all_gather | solution.py:103
  314.7 12.6 %convolution_add_fusion.1 = f32[160,1536]{1,0:T(8,128)} fusion(bf16[160,7168]{1,0:T(8,128)(2,1)} %constant_dynamic-update-slice_fusion, bf16[7168,1536]{1,0:T(8,128)(2,1)} %all-gather.10.cloned.1.call-done, f32[1536]{0:T(1024)S(1)} %convert_element_type.65), kind=kOutput, calls=%fused_computation.8 | convolution fusion | flops 3523461120 | bytes 25303040 | tf_op jit(solution)/shard_map/dot_general | solution.py:101
  327.4 4.2 convolution_add_fusion
  331.6 2.6 reshape.328
  334.2 2.8 fusion.45
  337.0 2.3 fusion.47
  339.3 1.5 fusion.12
  340.8 0.7 copy.40
  341.5 0.0 all-gather.12.cloned.1.call-update
  341.5 0.7 constant_dynamic-slice_fusion
  342.3 14.2 %all-gather = bf16[1,16,4096]{2,1,0:T(8,128)(2,1)S(1)} all-gather(bf16[1,16,512]{2,1,0:T(8,128)(2,1)S(1)} %constant_dynamic-slice_fusion), channel_id=2, replica_groups=mesh['row'=4,'col'=8] {'col'}, dimensions={2}, use_global_device_ids=true | all-gather | bytes 147456 | tf_op jit(solution)/shard_map/all_gather | solution.py:126
  356.5 38.9 %all-gather.14.cloned.1.call-done = bf16[4096,896]{1,0:T(8,128)(2,1)} async-done(((bf16[1024,896]{1,0:T(8,128)(2,1)}), bf16[4096,896]{1,0:T(8,128)(2,1)}) %all-gather.14.cloned.1.call-update) | async-done | bytes 7340048 | tf_op jit(solution)/shard_map/all_gather | solution.py:134
  395.4 24.9 %all-gather.12.cloned.1.call-done = bf16[160,4096]{1,0:T(8,128)(2,1)} async-done(((bf16[160,512]{1,0:T(8,128)(2,1)}), bf16[160,4096]{1,0:T(8,128)(2,1)}) %all-gather.12.cloned.1.call-update) | async-done | bytes 1310736 | tf_op jit(solution)/shard_map/all_gather | solution.py:125
  420.3 5.8 %convolution_add_fusion.3 = f32[160,896]{1,0:T(8,128)} fusion(bf16[160,4096]{1,0:T(8,128)(2,1)} %all-gather.12.cloned.1.call-done, bf16[4096,896]{1,0:T(8,128)(2,1)} %all-gather.14.cloned.1.call-done, f32[896]{0:T(1024)S(1)} %convert_element_type.75), kind=kOutput, calls=%fused_computation.19 | convolution fusion | flops 1174548480 | bytes 9227776 | tf_op jit(solution)/shard_map/dot_general | solution.py:132
  426.1 3.0 fusion.11
  (33 shorter events, 0.2 us)
Async XLA Ops:
  6.5 320.8 %copy-start = (bf16[64,16,1536]{2,1,0:T(8,128)(2,1)S(1)}, bf16[64,16,1536]{2,1,0:T(8,128)(2,1)}, u32[]{:S(2)}) copy-start(bf16[64,16,1536]{2,1,0:T(8,128)(2,1)} %param.24) | copy-start | bytes 9437188
  6.5 33.0 %all-gather.8.cloned.1.call-start = ((), (), s32[]{:S(2)}) async-start(), calls=%async_computation | async-start | bytes 1433600 | tf_op jit(solution)/shard_map/all_gather | solution.py:77
  7.3 104.6 %all-reduce.3.cloned.1.call-start = ((), (), s32[]{:S(2)}) async-start(), calls=%async_computation.4 | async-start | bytes 4587520 | tf_op jit(solution)/shard_map/psum | solution.py:13
  39.5 3.4 copy-start.2
  45.0 1.4 copy-start.7
  45.0 1.5 copy-start.1
  45.1 269.7 %all-gather.10.cloned.1.call-start = ((), (), s32[]{:S(2)}) async-start(), calls=%async_computation.1 | async-start | bytes 27525120 | tf_op jit(solution)/shard_map/all_gather | solution.py:103
  45.8 3.2 copy-start.4
  45.8 3.2 copy-start.8
  45.8 3.8 copy-start.6
  45.8 4.6 %copy-start.9 = (s32[4]{0:T(128)S(1)}, s32[4]{0:T(128)}, u32[]{:S(2)}) copy-start(s32[4]{0:T(128)} %param.27) | copy-start | bytes 52
  45.8 349.5 %all-gather.14.cloned.1.call-start = ((), (), s32[]{:S(2)}) async-start(), calls=%async_computation.3 | async-start | bytes 9175040 | tf_op jit(solution)/shard_map/all_gather | solution.py:134
  46.4 373.9 %all-gather.12.cloned.1.call-start = ((), (), s32[]{:S(2)}) async-start(), calls=%async_computation.2 | async-start | bytes 1474560 | tf_op jit(solution)/shard_map/all_gather | solution.py:125
  111.9 2.5 copy-start.3
  337.0 4.5 %copy-start.5 = (bf16[896]{0:T(1024)(128)(2,1)S(1)}, bf16[896]{0:T(1024)(128)(2,1)}, u32[]{:S(2)}) copy-start(bf16[896]{0:T(1024)(128)(2,1)} %param.22) | copy-start | bytes 5380
Sparse Core Ops, SparseCore 0:
  9.2 30.2 all-gather.7
  45.1 66.7 all-reduce.2
  113.8 200.9 all-gather.9
  316.4 78.8 all-gather.13
  396.8 23.4 all-gather.11
where the time goes:
time: 436 us
  waiting for transfers between devices  318 us (73%)
  blocking collectives  46 us (11%)
  matrix products  29.6 us (7%)
  between operations  15.3 us (4%)
  local copies, waits for them, and re-layouts  14.4 us (3%)
  other arithmetic  12.6 us (3%)
    all_gather x1, waiting for transfers between devices, local(): lax.all_gather(qkv_weight, 'row', axis=0, tiled=True)  199 us
    psum x1, waiting for transfers between devices, broadcast(): return lax.psum(jnp.where(mine, x, jnp.zeros_like(x)), axis)  39.9 us
    all_gather x1, waiting for transfers between devices, local(): lax.all_gather(out_weight, 'row', axis=0, tiled=True)  38.9 us
    all_gather x1, waiting for transfers between devices, local(): lax.all_gather(mixed_rows, 'col', axis=1, tiled=True)  24.9 us
    all_gather x1, blocking collectives, local(): lax.all_gather(down_here, 'col', axis=1, tiled=True)  14.2 us
    all_gather x1, blocking collectives, local(): lax.all_gather(lowered, 'row', axis=0, tiled=True)  14.1 us
    all_gather x1, waiting for transfers between devices, local(): lax.all_gather(hidden, 'row', axis=1, tiled=True)  12.8 us
    dot_general x1, matrix products, local(): jnp.dot(sliced, lax.all_gather(qkv_weight, 'row', axis=0, tiled=True), pr...  12.6 us
  transfers between devices with their start and end apart: 5, of which 5 were waited for; matrix products, arithmetic and copies ran while one was open for 10% of the time, Pallas kernels for 0%

commit v1 on v0

--- a/solution.py
+++ b/solution.py
@@ -6,11 +6,6 @@
 HEAD_SIZE = 128
 GCAP = 160
 WIN = 53
-
-
-def broadcast(x, axis, root):
-    mine = lax.axis_index(axis) == root
-    return lax.psum(jnp.where(mine, x, jnp.zeros_like(x)), axis)
 
 
 def group_layout(prompt, count, suffix):
@@ -50,6 +45,29 @@
     return mixed_rows.astype(jnp.bfloat16).reshape(queries.shape[0], -1)
 
 
+def normalise(hidden, ln_gain, ln_shift):
+    widened = hidden.astype(jnp.float32)
+    width = widened.shape[1]
+    own_mean = jnp.mean(widened, axis=1, keepdims=True)
+    centred = widened - own_mean
+    own_spread = jnp.sum(centred * centred, axis=1, keepdims=True)
+    every = lax.all_gather(jnp.concatenate([own_mean, own_spread], axis=1), "row", axis=0)
+    means, spreads = every[:, :, :1], every[:, :, 1:]
+    average = jnp.mean(means, axis=0)
+    between = jnp.sum((means - average) * (means - average), axis=0) * width
+    spread = (jnp.sum(spreads, axis=0) + between) / (width * every.shape[0])
+    return (
+        (widened - average) * lax.rsqrt(spread + 1e-05) * ln_gain.astype(jnp.float32)
+        + ln_shift.astype(jnp.float32)
+    ).astype(jnp.bfloat16)
+
+
+def sum_over_row(partial):
+    moved = lax.all_to_all(partial, "row", split_axis=0, concat_axis=0, tiled=True)
+    blocks = moved.reshape((lax.axis_size("row"), -1) + moved.shape[1:])
+    return jnp.sum(blocks.astype(jnp.float32), axis=0)
+
+
 def local(
     hidden,
     ln_gain,
@@ -69,47 +87,23 @@
     chosen,
 ):
     row_index = lax.axis_index("row")
-    row_count = lax.axis_size("row")
+    groups = lax.axis_size("row")
     adapters = chosen[group_adapter_choice]
     own_adapter = adapters[row_index]
-    low_rank = down_qkv.shape[2]
-    features, gain_full, shift_full = (
-        lax.all_gather(hidden, "row", axis=1, tiled=True),
-        lax.all_gather(ln_gain, "row", axis=0, tiled=True),
-        lax.all_gather(ln_shift, "row", axis=0, tiled=True),
-    )
-    widened = features.astype(jnp.float32)
-    average = jnp.mean(widened, axis=1, keepdims=True)
-    centred = widened - average
-    spread = jnp.mean(centred * centred, axis=1, keepdims=True)
-    normed = (
-        centred * lax.rsqrt(spread + 1e-05) * gain_full.astype(jnp.float32)
-        + shift_full.astype(jnp.float32)
-    ).astype(jnp.bfloat16)
-    per_group = lax.axis_size("col") // row_count
-    received = []
-    for offset in range(per_group):
-        received.append(broadcast(normed, "col", row_index * per_group + offset))
-    group_rows = jnp.concatenate(received, axis=0)
-    lowered = jnp.transpose(down_qkv[adapters], (1, 0, 2)).reshape(
-        down_qkv.shape[1], row_count * low_rank
-    )
-    sliced = group_rows
-    own_down = lax.dynamic_slice_in_dim(
-        lax.all_gather(lowered, "row", axis=0, tiled=True), row_index * low_rank, low_rank, 1
-    )
-    projected = jnp.dot(
-        sliced,
-        lax.all_gather(qkv_weight, "row", axis=0, tiled=True),
+    normed = normalise(hidden, ln_gain, ln_shift)
+    tokens = lax.all_gather(normed, "col", axis=0, tiled=True)
+    low_part = jnp.einsum(
+        "gtd,gdr->gtr",
+        tokens.reshape(groups, GCAP, -1),
+        down_qkv[adapters],
         preferred_element_type=jnp.float32,
     )
-    reduced = jnp.dot(sliced, own_down, preferred_element_type=jnp.float32)
+    low = sum_over_row(low_part.reshape(groups * GCAP, -1)).astype(jnp.bfloat16)
+    part = jnp.dot(tokens, qkv_weight, preferred_element_type=jnp.float32).astype(jnp.bfloat16)
     projected = (
-        projected
+        sum_over_row(part)
         + qkv_bias.astype(jnp.float32)
-        + jnp.dot(
-            reduced.astype(jnp.bfloat16), up_qkv[own_adapter], preferred_element_type=jnp.float32
-        )
+        + jnp.dot(low, up_qkv[own_adapter], preferred_element_type=jnp.float32)
     )
     heads_here = projected.shape[1] // (3 * HEAD_SIZE)
     shaped = projected.reshape(GCAP, heads_here, 3, HEAD_SIZE)
@@ -120,22 +114,15 @@
         prompt_lens[row_index], group_sizes[row_index], suffix_lens[row_index]
     )
     mixed_rows = attention(queries, key_rows, value_rows, key_mask(live_rows, request_of, position))
-    down_here = down_out[own_adapter]
-    all_heads, down_full = (
-        lax.all_gather(mixed_rows, "col", axis=1, tiled=True),
-        lax.all_gather(down_here, "col", axis=1, tiled=True),
-    )
+    all_heads = lax.all_gather(mixed_rows, "col", axis=1, tiled=True)
+    down_full = lax.all_gather(down_out[own_adapter], "col", axis=1, tiled=True)
     reduced_out = lax.dot_general(
         all_heads, down_full, (((1,), (1,)), ((), ())), preferred_element_type=jnp.float32
     ).astype(jnp.bfloat16)
-    sliced = all_heads
-    combined = jnp.dot(
-        sliced,
-        lax.all_gather(out_weight, "row", axis=0, tiled=True),
-        preferred_element_type=jnp.float32,
-    )
+    gathered = lax.all_to_all(all_heads, "row", split_axis=1, concat_axis=0, tiled=True)
+    out_part = jnp.dot(gathered, out_weight, preferred_element_type=jnp.float32)
     result = (
-        combined
+        sum_over_row(out_part.astype(jnp.bfloat16))
         + out_bias.astype(jnp.float32)
         + jnp.dot(reduced_out, up_out[own_adapter], preferred_element_type=jnp.float32)
     )

time: 436 us -> 189 us (0.43)
  waiting for transfers between devices: 318 us -> 65 us
  starting transfers between devices: 0.16 us -> 12.7 us
  matrix products: 29.6 us -> 21.9 us
  other arithmetic: 12.6 us -> 17.9 us
    all_gather x4 -> x2, waiting for transfers between devices: 276 us -> 49.4 us  [the longest x1 27.2 us: local(): tokens = lax.all_gather(normed, 'col', axis=0, tiled=True)]
    psum x1 -> x0, waiting for transfers between devices: 39.9 us -> none  [broadcast(): return lax.psum(jnp.where(mine, x, jnp.zeros_like(x)), axis)]
    all_gather x4 -> x2, blocking collectives: 46 us -> 23.5 us  [the longest x1 13.9 us: local(): down_full = lax.all_gather(down_out[own_adapter], 'col', axis=1, tiled=True)]
    all_to_all x0 -> x1, blocking collectives: none -> 20.9 us  [local(): lax.all_to_all(all_heads, 'row', split_axis=1, concat_axis=0, tiled=True)]
    all_to_all x0 -> x3, waiting for transfers between devices: none -> 15.6 us  [sum_over_row(): lax.all_to_all(partial, 'row', split_axis=0, concat_axis=0, tiled=True)]
    all_to_all x0 -> x3, starting transfers between devices: none -> 12.6 us  [sum_over_row(): lax.all_to_all(partial, 'row', split_axis=0, concat_axis=0, tiled=True)]
    dot_general x3 -> x4, matrix products: 22.7 us -> 15.1 us  [the longest x1 8.24 us: local(): jnp.dot(tokens, qkv_weight, preferred_element_type=jnp.float32)]
  transfers between devices with their start and end apart: 5 -> 5, of which waited for: 5 -> 3; matrix products, arithmetic and copies ran while one was open for 10% -> 10% of each run, Pallas kernels for 0% -> 0%
where the time goes in v1:
time: 189 us; the launch traced here: 188 us
  waiting for transfers between devices  65 us (34%)
  blocking collectives  44.4 us (23%)
  matrix products  21.9 us (12%)
  other arithmetic  17.9 us (9%)
  between operations  15.5 us (8%)
  starting transfers between devices  12.7 us (7%)
  local copies, waits for them, and re-layouts  10.7 us (6%)
    all_gather x1, waiting for transfers between devices, local(): tokens = lax.all_gather(normed, 'col', axis=0, tiled=True)  27.2 us
    all_gather x1, waiting for transfers between devices, local(): all_heads = lax.all_gather(mixed_rows, 'col', axis=1, tiled=True)  22.1 us
    all_to_all x1, blocking collectives, local(): lax.all_to_all(all_heads, 'row', split_axis=1, concat_axis=0, tiled=True)  20.9 us
    all_to_all x3, waiting for transfers between devices, sum_over_row(): lax.all_to_all(partial, 'row', split_axis=0, concat_axis=0, tiled=True)  15.6 us
    all_gather x1, blocking collectives, local(): down_full = lax.all_gather(down_out[own_adapter], 'col', axis=1, tiled=True)  13.9 us
    all_to_all x3, starting transfers between devices, sum_over_row(): lax.all_to_all(partial, 'row', split_axis=0, concat_axis=0, tiled=True)  12.6 us
    all_gather x1, blocking collectives, normalise(): lax.all_gather(jnp.concatenate([own_mean, own_spread], axis=1), 'row', ax...  9.52 us
    dot_general x1, matrix products, local(): jnp.dot(tokens, qkv_weight, preferred_element_type=jnp.float32)  8.24 us
  transfers between devices with their start and end apart: 5, of which 3 were waited for; matrix products, arithmetic and copies ran while one was open for 10% of the time, Pallas kernels for 0%

profile of v1, /device:TPU:0, one launch (start us, length us, event | category | flops | bytes accessed | tf_op | source)
XLA Modules:
  0.0 188.0 jit_solution(3416726104316750759)
XLA Ops:
  6.5 1.3 convert_reduce_fusion.2
  7.8 1.2 fusion.8
  9.0 9.5 %all-gather.2 = f32[4,80,2]{1,2,0:T(2,128)S(1)} all-gather(f32[1,80,2]{1,2,0:T(2,128)S(1)} %maximum_bitcast_fusion), channel_id=2, replica_groups=mesh['row'=4,'col'=8] {'row'}, dimensions={0}, use_global_device_ids=true | all-gather | bytes 3200 | tf_op jit(solution)/shard_map/all_gather | solution.py:54
  18.6 0.7 convert_element_type.74
  19.3 0.7 convert_element_type.75
  20.0 1.9 %fusion.12 = bf16[80,1792]{1,0:T(8,128)(2,1)} fusion(bf16[80,1792]{1,0:T(8,128)(2,1)} %param.16, f32[1792]{0:T(1024)S(1)} %convert_element_type.75, f32[1792]{0:T(1024)S(1)} %convert_element_type.74, f32[80]{0:T(128)S(1)} %add_rsqrt_fusion, f32[80]{0:T(128)S(1)} %broadcast_multiply_fusion), kind=kLoop, calls=%fused_computation.28 | loop fusion | flops 860160 | bytes 588416 | tf_op jit(solution)/shard_map/convert_element_type | solution.py:62
  21.9 0.0 all-gather.6.cloned.1.call-update
  21.9 0.7 compare_select_fusion.1
  22.6 0.6 gather_fusion
  23.2 2.6 %gather_fusion.1 = bf16[4,1792,16]{1,2,0:T(8,128)(2,1)S(1)} fusion(bf16[64,1792,16]{1,2,0:T(8,128)(2,1)} %param.23, s32[1024]{0:T(1024)S(1)} %pad_clamp_fusion), kind=kCustom, calls=%fused_computation.1 | custom fusion | bytes 458768 | tf_op jit(solution)/shard_map/gather | solution.py:98
  25.8 27.2 %all-gather.6.cloned.1.call-done = bf16[640,1792]{1,0:T(8,128)(2,1)} async-done(((bf16[80,1792]{1,0:T(8,128)(2,1)}), bf16[640,1792]{1,0:T(8,128)(2,1)}) %all-gather.6.cloned.1.call-update) | async-done | bytes 2293776 | tf_op jit(solution)/shard_map/all_gather | solution.py:94
  53.1 3.0 %fusion.49 = f32[4,160,16]{1,2,0:T(8,128)} fusion(bf16[4,160,1792]{2,1,0:T(8,128)(2,1)} %bitcast.77, bf16[4,1792,16]{1,2,0:T(8,128)(2,1)S(1)} %gather_fusion.1), kind=kOutput, calls=%fused_computation.86 | convolution fusion | flops 36700160 | bytes 2564096 | tf_op jit(solution)/shard_map/gtd,gdr->gtr/dot_general | solution.py:95
  56.1 3.6 %all-to-all-start.1 = ((f32[4,160,16]{1,2,0:T(8,128)}), f32[4,160,16]{1,2,0:T(8,128)S(1)}, u32[]{:S(2)}, u32[]{:S(2)}) async-start(f32[4,160,16]{1,2,0:T(8,128)} %fusion.49), calls=%async_computation.1 | async-start | bytes 131072 | tf_op jit(solution)/shard_map/all_to_all | solution.py:66
  59.7 8.2 %convolution_convert_fusion = bf16[640,1536]{1,0:T(8,128)(2,1)} fusion(bf16[640,1792]{1,0:T(8,128)(2,1)} %all-gather.6.cloned.1.call-done, bf16[1792,1536]{1,0:T(8,128)(2,1)} %param.19), kind=kOutput, calls=%fused_computation.4 | convolution fusion | flops 3524198400 | bytes 9764864 | tf_op jit(solution)/shard_map/dot_general | solution.py:102
  68.0 0.0 copy-start.7
  68.0 0.0 copy-start.2
  68.0 4.6 %all-to-all-start = ((bf16[4,160,1536]{2,1,0:T(8,128)(2,1)}), bf16[4,160,1536]{2,1,0:T(8,128)(2,1)}, u32[]{:S(2)}, u32[]{:S(2)}) async-start(bf16[4,160,1536]{2,1,0:T(8,128)(2,1)} %bitcast.78), calls=%async_computation | async-start | bytes 3932160 | tf_op jit(solution)/shard_map/all_to_all | solution.py:66
  72.6 0.0 all-gather.8.cloned.1.call-start
  72.6 0.7 dynamic_slice.21
  73.3 0.6 dynamic_slice.24
  73.8 0.7 compare_select_fusion.3
  74.5 0.1 copy.40
  74.6 0.6 dynamic_slice.23
  77.1 0.7 add_reduce_fusion
  77.9 0.1 convert_reduce_fusion.3
  78.0 0.7 fusion.34
  78.6 0.1 select_reduce_fusion
  78.7 0.6 broadcast_compare_fusion
  79.4 1.3 fusion.43
  80.7 0.2 fusion.19
  80.9 15.6 %all-to-all-done = bf16[4,160,1536]{2,1,0:T(8,128)(2,1)} async-done(((bf16[4,160,1536]{2,1,0:T(8,128)(2,1)}), bf16[4,160,1536]{2,1,0:T(8,128)(2,1)}, u32[]{:S(2)}, u32[]{:S(2)}) %all-to-all-start) | async-done | bytes 1966112 | tf_op jit(solution)/shard_map/all_to_all | solution.py:66
  96.5 2.0 %convert_reduce_fusion = f32[160,1536]{1,0:T(8,128)S(1)} fusion(bf16[4,160,1536]{2,1,0:T(8,128)(2,1)} %all-to-all-done), kind=kLoop, calls=%fused_computation.3 | loop fusion | flops 1720320 | bytes 2949120 | tf_op jit(solution)/shard_map/reduce_sum | solution.py:68
  98.5 1.3 convolution_add_fusion
  99.8 2.6 %reshape.370 = f32[160,4,3,128]{3,2,1,0:T(4,128)} reshape(f32[160,1536]{1,0:T(8,128)} %convolution_add_fusion) | data formatting | bytes 1966080 | tf_op jit(solution)/shard_map/reshape | solution.py:109
  102.4 2.8 %fusion.44 = (bf16[160,4,3,128]{3,0,1,2:T(8,128)(2,1)}, f32[160,4,3,128]{3,0,1,2:T(8,128)}) fusion(f32[160,4,3,128]{3,2,1,0:T(4,128)} %reshape.370), kind=kLoop, calls=%fused_computation.84 | loop fusion | flops 245760 | bytes 2457600 | tf_op jit(solution)/shard_map/convert.1
  105.2 2.3 %fusion.46 = (f32[4,160]{1,0:T(4,128)S(1)}, f32[4,160,160]{1,2,0:T(8,128)}) fusion(pred[160,160]{0,1:T(8,128)(4,1)S(1)} %fusion.19, f32[160,4,3,128]{3,0,1,2:T(8,128)} %get-tuple-element.10, bf16[160,4,3,128]{3,0,1,2:T(8,128)(2,1)} %get-tuple-element.9), kind=kOutput, calls=%fused_computation.85 | convolution fusion | flops 26788000 | bytes 985600 | tf_op jit(solution)/shard_map/sub | solution.py:42
  107.4 1.5 fusion.6
  108.9 0.7 copy.52
  109.6 0.0 all-gather.8.cloned.1.call-update
  109.7 22.1 %all-gather.8.cloned.1.call-done = bf16[160,4096]{1,0:T(8,128)(2,1)} async-done(((bf16[160,512]{1,0:T(8,128)(2,1)}), bf16[160,4096]{1,0:T(8,128)(2,1)}) %all-gather.8.cloned.1.call-update) | async-done | bytes 1310736 | tf_op jit(solution)/shard_map/all_gather | solution.py:117
  131.8 1.4 copy.51
  133.2 20.9 %all_to_all.43 = bf16[160,4,1024]{2,0,1:T(8,128)(2,1)S(1)} all-to-all(bf16[160,4,1024]{2,0,1:T(8,128)(2,1)S(1)} %bitcast.76), channel_id=1, replica_groups=mesh['row'=4,'col'=8] {'row'}, dimensions={1} | all-to-all | bytes 2621440 | tf_op jit(solution)/shard_map/all_to_all | solution.py:122
  154.2 2.5 %convolution_convert_fusion.1 = bf16[640,896]{1,0:T(8,128)(2,1)} fusion(bf16[640,1024]{1,0:T(8,128)(2,1)S(1)} %bitcast.79, bf16[1024,896]{1,0:T(8,128)(2,1)S(1)} %copy-done.5), kind=kOutput, calls=%fused_computation.7 | convolution fusion | flops 1174978560 | bytes 4292608 | tf_op jit(solution)/shard_map/dot_general | solution.py:123
  156.7 4.4 %all-to-all-start.3 = ((bf16[4,160,896]{2,1,0:T(8,128)(2,1)}), bf16[4,160,896]{2,1,0:T(8,128)(2,1)}, u32[]{:S(2)}, u32[]{:S(2)}) async-start(bf16[4,160,896]{2,1,0:T(8,128)(2,1)} %bitcast.80), calls=%async_computation.3 | async-start | bytes 2293760 | tf_op jit(solution)/shard_map/all_to_all | solution.py:66
  161.2 0.7 constant_dynamic-slice_fusion
  161.9 13.9 %all-gather.1 = bf16[1,16,4096]{2,1,0:T(8,128)(2,1)S(1)} all-gather(bf16[1,16,512]{2,1,0:T(8,128)(2,1)S(1)} %constant_dynamic-slice_fusion), channel_id=3, replica_groups=mesh['row'=4,'col'=8] {'col'}, dimensions={2}, use_global_device_ids=true | all-gather | bytes 147456 | tf_op jit(solution)/shard_map/all_gather | solution.py:118
  175.8 2.3 %convert_reduce_fusion.1 = f32[160,896]{1,0:T(8,128)} fusion(bf16[4,160,896]{2,1,0:T(8,128)(2,1)} %all-to-all-done.3), kind=kLoop, calls=%fused_computation.6 | loop fusion | flops 1003520 | bytes 1720320 | tf_op jit(solution)/shard_map/reduce_sum | solution.py:68
  178.1 3.0 %fusion.5 = bf16[160,896]{1,0:T(8,128)(2,1)} fusion(bf16[160,4096]{1,0:T(8,128)(2,1)} %all-gather.8.cloned.1.call-done, f32[160,896]{1,0:T(8,128)} %convert_reduce_fusion.1, f32[160]{0:T(256)S(1)} %get-tuple-element.7, f32[896]{0:T(1024)S(1)} %convert_element_type.91, bf16[1,16,4096]{2,1,0:T(8,128)(2,1)S(1)} %all-gather.1, bf16[64,16,896]{2,1,0:T(8,128)(2,1)} %param.26, ...), kind=kOutput, calls=%fused_computation.15 | convolution fusion | flops 26135040 | bytes 2334852 | tf_op jit(solution)/shard_map/dot_general | solution.py:127
  (30 shorter events, 0.2 us)
Async XLA Ops:
  6.5 91.9 %copy-start = (bf16[64,16,1536]{2,1,0:T(8,128)(2,1)S(1)}, bf16[64,16,1536]{2,1,0:T(8,128)(2,1)}, u32[]{:S(2)}) copy-start(bf16[64,16,1536]{2,1,0:T(8,128)(2,1)} %param.24) | copy-start | bytes 9437188
  6.5 16.0 %copy-start.1 = (s32[16]{0:T(128)S(1)}, s32[16]{0:T(128)}, u32[]{:S(2)}) copy-start(s32[16]{0:T(128)} %param.31) | copy-start | bytes 196
  6.5 46.6 %all-gather.6.cloned.1.call-start = ((), (), s32[]{:S(2)}) async-start(), calls=%async_computation.4 | async-start | bytes 2580480 | tf_op jit(solution)/shard_map/all_gather | solution.py:94
  56.1 11.9 %all-to-all-start.1 = ((f32[4,160,16]{1,2,0:T(8,128)}), f32[4,160,16]{1,2,0:T(8,128)S(1)}, u32[]{:S(2)}, u32[]{:S(2)}) async-start(f32[4,160,16]{1,2,0:T(8,128)} %fusion.49), calls=%async_computation.1 | async-start | bytes 131072 | tf_op jit(solution)/shard_map/all_to_all | solution.py:66
  68.0 5.3 %copy-start.6 = (s32[4]{0:T(128)S(1)}, s32[4]{0:T(128)}, u32[]{:S(2)}) copy-start(s32[4]{0:T(128)} %param.29) | copy-start | bytes 52
  68.0 5.9 %copy-start.4 = (s32[4,16]{1,0:T(4,128)S(1)}, s32[4,16]{1,0:T(4,128)}, u32[]{:S(2)}) copy-start(s32[4,16]{1,0:T(4,128)} %param.28) | copy-start | bytes 772
  68.0 6.7 %copy-start.7 = (s32[4]{0:T(128)S(1)}, s32[4]{0:T(128)}, u32[]{:S(2)}) copy-start(s32[4]{0:T(128)} %param.27) | copy-start | bytes 52
  68.0 8.5 %copy-start.2 = (bf16[1536]{0:T(1024)(128)(2,1)S(1)}, bf16[1536]{0:T(1024)(128)(2,1)}, u32[]{:S(2)}) copy-start(bf16[1536]{0:T(1024)(128)(2,1)} %param.20) | copy-start | bytes 9220
  68.0 28.5 %all-to-all-start = ((bf16[4,160,1536]{2,1,0:T(8,128)(2,1)}), bf16[4,160,1536]{2,1,0:T(8,128)(2,1)}, u32[]{:S(2)}, u32[]{:S(2)}) async-start(bf16[4,160,1536]{2,1,0:T(8,128)(2,1)} %bitcast.78), calls=%async_computation | async-start | bytes 3932160 | tf_op jit(solution)/shard_map/all_to_all | solution.py:66
  72.6 59.3 %all-gather.8.cloned.1.call-start = ((), (), s32[]{:S(2)}) async-start(), calls=%async_computation.5 | async-start | bytes 1474560 | tf_op jit(solution)/shard_map/all_gather | solution.py:117
  133.2 20.9 %copy-start.5 = (bf16[1024,896]{1,0:T(8,128)(2,1)S(1)}, bf16[1024,896]{1,0:T(8,128)(2,1)}, u32[]{:S(2)}) copy-start(bf16[1024,896]{1,0:T(8,128)(2,1)} %param.21) | copy-start | bytes 5505028
  156.7 4.4 %copy-start.3 = (bf16[896]{0:T(1024)(128)(2,1)S(1)}, bf16[896]{0:T(1024)(128)(2,1)}, u32[]{:S(2)}) copy-start(bf16[896]{0:T(1024)(128)(2,1)} %param.22) | copy-start | bytes 5380
  156.7 19.1 %all-to-all-start.3 = ((bf16[4,160,896]{2,1,0:T(8,128)(2,1)}), bf16[4,160,896]{2,1,0:T(8,128)(2,1)}, u32[]{:S(2)}, u32[]{:S(2)}) async-start(bf16[4,160,896]{2,1,0:T(8,128)(2,1)} %bitcast.80), calls=%async_computation.3 | async-start | bytes 2293760 | tf_op jit(solution)/shard_map/all_to_all | solution.py:66
Sparse Core Ops, SparseCore 0:
  22.0 31.0 all-gather.5
  109.8 21.9 all-gather.7

commit v2 on v1

--- a/solution.py
+++ b/solution.py
@@ -1,6 +1,10 @@
+import functools
+
 import jax
 import jax.numpy as jnp
 from jax import lax
+from jax.experimental import pallas as pl
+from jax.experimental.pallas import tpu as pltpu
 from jax.sharding import PartitionSpec as P
 
 HEAD_SIZE = 128
@@ -129,6 +133,617 @@
     return (result * live_rows[:, None].astype(jnp.float32)).astype(jnp.bfloat16)
 
 
+HIDDEN_PART = 3 * HEAD_SIZE
+BF = jnp.bfloat16
+F32 = jnp.float32
+
+
+def fused_kernel(
+    planes,
+    hidden,
+    gain,
+    shift,
+    qkv_bias,
+    out_bias,
+    prompt_lens,
+    suffix_lens,
+    group_sizes,
+    choice,
+    chosen,
+    qkv_hbm,
+    out_hbm,
+    down_qkv_hbm,
+    up_qkv_hbm,
+    down_out_hbm,
+    up_out_hbm,
+    out,
+    qkv_w,
+    out_w,
+    down_qkv,
+    up_qkv,
+    down_out,
+    up_out,
+    stats,
+    x,
+    part_out,
+    part_in,
+    part_own,
+    low_own,
+    low_in,
+    mixed_out,
+    mixed,
+    res_out,
+    res_in,
+    res_own,
+    lowo_out,
+    lowo_in,
+    lowo_own,
+    load_sem,
+    stat_send,
+    stat_recv,
+    x_send,
+    x_recv,
+    part_send,
+    part_recv,
+    low_send,
+    low_recv,
+    mixed_send,
+    mixed_recv,
+    chain_send,
+    chain_recv,
+    res_send,
+    res_recv,
+    lowo_send,
+    lowo_recv,
+):
+    rows = planes
+    r = lax.axis_index("row")
+    c = lax.axis_index("col")
+    z = c // 2
+    k = c % 2
+    sib = c + 1 - 2 * k
+    block = hidden.shape[0]
+    head_col = pl.multiple_of(r * HIDDEN_PART, 128)
+
+    def to(src, dst, send, recv, row, col):
+        return pltpu.make_async_remote_copy(
+            src_ref=src,
+            dst_ref=dst,
+            send_sem=send,
+            recv_sem=recv,
+            device_id=(row, col),
+            device_id_type=pl.DeviceIdType.MESH,
+        )
+
+    loads = [
+        pltpu.make_async_copy(qkv_hbm, qkv_w, load_sem.at[0]),
+        pltpu.make_async_copy(down_qkv_hbm, down_qkv, load_sem.at[1]),
+        pltpu.make_async_copy(
+            up_qkv_hbm.at[:, :, pl.ds(head_col, HIDDEN_PART)], up_qkv, load_sem.at[2]
+        ),
+        pltpu.make_async_copy(down_out_hbm, down_out, load_sem.at[3]),
+        pltpu.make_async_copy(out_hbm, out_w, load_sem.at[4]),
+        pltpu.make_async_copy(up_out_hbm, up_out, load_sem.at[5]),
+    ]
+    for load in loads:
+        load.start()
+
+    barrier = pltpu.get_barrier_semaphore()
+
+    def greet(row, col):
+        pl.semaphore_signal(
+            barrier, inc=1, device_id=(row, col), device_id_type=pl.DeviceIdType.MESH
+        )
+
+    greet(r, sib)
+    for step in range(1, rows):
+        greet((r + step) % rows, c)
+
+    @pl.when(z > 0)
+    def _():
+        greet(r, c - 2)
+
+    @pl.when(z < planes - 1)
+    def _():
+        greet(r, c + 2)
+
+    before = (z + planes - 1) // planes
+    after = (2 * planes - 2 - z) // planes
+    pl.semaphore_wait(barrier, rows + before + after)
+
+    wide = hidden[...].astype(F32)
+    width = wide.shape[1]
+    own_mean = jnp.mean(wide, axis=1, keepdims=True)
+    centred = wide - own_mean
+    own_spread = jnp.sum(centred * centred, axis=1, keepdims=True)
+    lane = lax.broadcasted_iota(jnp.int32, (block, 128), 1)
+    stats[r] = jnp.where(lane == 0, own_mean, own_spread)
+
+    def stat_copy(row):
+        return to(stats.at[r], stats.at[r], stat_send.at[row], stat_recv.at[r], row, c)
+
+    for step in range(1, rows):
+        stat_copy((r + step) % rows).start()
+    for step in range(1, rows):
+        peer = (r + step) % rows
+        to(stats.at[peer], stats.at[peer], stat_send.at[peer], stat_recv.at[peer], r, c).wait_recv()
+    means = [stats[i][:, 0:1] for i in range(rows)]
+    average = sum(means) / rows
+    spread = sum(stats[i][:, 1:2] for i in range(rows))
+    spread = spread + width * sum((m - average) * (m - average) for m in means)
+    spread = spread / (width * rows)
+
+    def x_rows(index):
+        return pl.ds(pl.multiple_of(index * block, 16), block)
+
+    x[x_rows(c), :] = (
+        (hidden[...].astype(F32) - average)
+        * lax.rsqrt(spread + 1e-05)
+        * gain[...].astype(F32)
+        + shift[...].astype(F32)
+    ).astype(BF)
+
+    def x_copy(way, group, col):
+        at = x_rows(2 * group + k)
+        return to(
+            x.at[at], x.at[at], x_send.at[way, group], x_recv.at[2 * group + k], r, col
+        )
+
+    def x_wait(index):
+        at = x_rows(index)
+        to(x.at[at], x.at[at], x_send.at[0, 0], x_recv.at[index], r, c).wait_recv()
+
+    def part_copy(group, row):
+        return to(
+            part_out.at[group, row],
+            part_in.at[group, r],
+            part_send.at[group, row],
+            part_recv.at[group, r],
+            row,
+            c,
+        )
+
+    def low_copy(group, row):
+        return to(
+            low_own.at[group],
+            low_in.at[group, r],
+            low_send.at[group, row],
+            low_recv.at[group, r],
+            row,
+            c,
+        )
+
+    def adapter(group):
+        return chosen[choice[group]]
+
+    def token_rows(group):
+        return pl.ds(pl.multiple_of(group * GCAP, 16), GCAP)
+
+    def project(group):
+        low_own[group] = lax.dot_general(
+            down_qkv[adapter(group)],
+            x[token_rows(group), :],
+            (((1,), (1,)), ((), ())),
+            preferred_element_type=F32,
+        )
+        for step in range(1, rows):
+            low_copy(group, (r + step) % rows).start()
+
+        def one(step, _):
+            row = (r + step) % rows
+            cols = pl.ds(pl.multiple_of(row * HIDDEN_PART, 128), HIDDEN_PART)
+            part = jnp.dot(
+                x[token_rows(group), :], qkv_w[:, cols], preferred_element_type=F32
+            )
+
+            @pl.when(row != r)
+            def _():
+                part_out[group, row] = part.astype(BF)
+                part_copy(group, row).start()
+
+            @pl.when(row == r)
+            def _():
+                part_own[group] = part
+
+            return 0
+
+        lax.fori_loop(1, rows + 1, one, 0)
+
+    def layout(group, axis):
+        shape = (GCAP, 1) if axis == 0 else (1, GCAP)
+        offsets = lax.broadcasted_iota(jnp.int32, shape, axis)
+        prompt = prompt_lens[group]
+        count = group_sizes[group]
+        end = prompt
+        request = jnp.zeros(shape, jnp.int32)
+        begin = jnp.zeros(shape, jnp.int32)
+        for j in range(suffix_lens.shape[1]):
+            start = end
+            end = end + jnp.where(j < count, suffix_lens[group, j], 0)
+            passed = jnp.where(offsets >= end, 1, 0)
+            begin = begin + jnp.where(offsets >= start, (1 - passed) * start, 0)
+            request = request + passed
+        inside = offsets < prompt
+        position = jnp.where(inside, offsets, prompt + offsets - begin)
+        request = jnp.where(inside, -1, jnp.where(request < count, request, -2))
+        return offsets, request, position
+
+    def allowed_of(group):
+        _, request_q, position_q = layout(group, 0)
+        key, request_k, position_k = layout(group, 1)
+        square = (GCAP, GCAP)
+        rq = jnp.broadcast_to(request_q, square)
+        rk = jnp.broadcast_to(request_k, square)
+        pq = jnp.broadcast_to(position_q, square)
+        pk = jnp.broadcast_to(position_k, square)
+        keys = jnp.broadcast_to(key, square)
+        shared = (rk == -1) | ((rk == rq) & (rk != -2))
+        near = (pq - pk < WIN) | (pk == 0)
+        live = shared & (pk <= pq) & near & (rq != -2)
+        return live | ((rq == -2) & (keys == 0))
+
+    def mixed_copy(group, row_from):
+        return to(
+            mixed_out.at[group],
+            mixed.at[group, k, pl.ds(0, GCAP), pl.ds(pl.multiple_of(row_from * 128, 128), 128)],
+            mixed_send.at[group],
+            mixed_recv.at[group, row_from],
+            z,
+            c,
+        )
+
+    def attend(group):
+        low = low_own[group]
+        proj = part_own[group] + qkv_bias[:, pl.ds(head_col, HIDDEN_PART)].astype(F32)
+        for step in range(1, rows):
+            peer = (r + step) % rows
+            to(
+                low_own.at[group], low_in.at[group, peer],
+                low_send.at[group, peer], low_recv.at[group, peer], r, c,
+            ).wait_recv()
+            low = low + low_in[group, peer]
+        for step in range(1, rows):
+            peer = (r + step) % rows
+            to(
+                part_out.at[group, peer], part_in.at[group, peer],
+                part_send.at[group, peer], part_recv.at[group, peer], r, c,
+            ).wait_recv()
+            proj = proj + part_in[group, peer].astype(F32)
+        proj = proj + lax.dot_general(
+            low.astype(BF), up_qkv[adapter(group)], (((0,), (0,)), ((), ())),
+            preferred_element_type=F32,
+        )
+        query = (proj[:, :HEAD_SIZE] * HEAD_SIZE ** (-0.5)).astype(BF)
+        key = proj[:, HEAD_SIZE : 2 * HEAD_SIZE].astype(BF)
+        value = proj[:, 2 * HEAD_SIZE :].astype(BF)
+        allowed = allowed_of(group)
+        scores = lax.dot_general(
+            query, key, (((1,), (1,)), ((), ())), preferred_element_type=F32
+        )
+        scores = jnp.where(allowed, scores, -1e30)
+        highest = jnp.max(scores, axis=1, keepdims=True)
+        weights = jnp.where(allowed, jnp.exp(scores - highest), 0.0)
+        probs = (weights / jnp.sum(weights, axis=1, keepdims=True)).astype(BF)
+        rows_mixed = jnp.dot(probs, value, preferred_element_type=F32).astype(BF)
+
+        @pl.when(r == z)
+        def _():
+            mixed[group, k, pl.ds(0, GCAP), pl.ds(pl.multiple_of(r * 128, 128), 128)] = rows_mixed
+            mixed[group, k, pl.ds(GCAP, 16), :] = down_out[adapter(group)]
+
+        @pl.when(r != z)
+        def _():
+            mixed_out[group] = rows_mixed
+            mixed_copy(group, r).start()
+
+    loads[0].wait()
+    loads[1].wait()
+    loads[2].wait()
+    loads[3].wait()
+
+    def first(step, _):
+        @pl.when(step < planes)
+        def _():
+            for side in range(2):
+                group = z + step * (2 * side - 1)
+                valid = (group >= 0) & (group < planes)
+                if side == 1:
+                    valid = valid & (step > 0)
+
+                @pl.when(valid)
+                def _():
+                    @pl.when(step > 0)
+                    def _():
+                        x_wait(2 * group + k)
+
+                    @pl.when((group <= z) & (z < planes - 1))
+                    def _():
+                        x_copy(0, group, c + 2).start()
+
+                    @pl.when((group >= z) & (z > 0))
+                    def _():
+                        x_copy(1, group, c - 2).start()
+
+                    x_copy(2, group, sib).start()
+
+            def compute(side, _):
+                group = z + step * (2 * side - 1)
+
+                @pl.when((group >= 0) & (group < planes) & (step + 1 - side > 0))
+                def _():
+                    x_wait(2 * group + 1 - k)
+                    project(group)
+
+                return 0
+
+            lax.fori_loop(0, 2, compute, 0)
+
+        @pl.when(step > 0)
+        def _():
+            def mix(side, _):
+                group = z + (step - 1) * (2 * side - 1)
+
+                @pl.when((group >= 0) & (group < planes) & (step - side > 0))
+                def _():
+                    attend(group)
+
+                return 0
+
+            lax.fori_loop(0, 2, mix, 0)
+
+        return 0
+
+    lax.fori_loop(0, planes + 1, first, 0)
+    loads[4].wait()
+    loads[5].wait()
+
+    def chain_copy(way, group, col):
+        return to(
+            mixed.at[group, k], mixed.at[group, k],
+            chain_send.at[way, group], chain_recv.at[group, k], r, col,
+        )
+
+    def chain_wait(group, half):
+        to(
+            mixed.at[group, half], mixed.at[group, half],
+            chain_send.at[0, group], chain_recv.at[group, half], r, c,
+        ).wait_recv()
+
+    def res_copy(group):
+        return to(res_out.at[group], res_in.at[r], res_send.at[group], res_recv.at[r], group, c)
+
+    def lowo_copy(group):
+        return to(
+            lowo_out.at[group], lowo_in.at[r], lowo_send.at[group], lowo_recv.at[r], group, c
+        )
+
+    half_rows = out_w.shape[0] // 2
+
+    def combine(group):
+        @pl.when(z == r)
+        def _():
+            for step in range(1, rows):
+                mixed_copy(group, (r + step) % rows).wait_recv()
+
+        @pl.when(z != r)
+        def _():
+            chain_wait(group, k)
+
+        @pl.when((z >= r) & (z < planes - 1))
+        def _():
+            chain_copy(0, group, c + 2).start()
+
+        @pl.when((z <= r) & (z > 0))
+        def _():
+            chain_copy(1, group, c - 2).start()
+
+        chain_copy(2, group, sib).start()
+        chain_wait(group, 1 - k)
+        low = jnp.zeros((16, GCAP), F32)
+        part = jnp.zeros((GCAP, out_w.shape[1]), F32)
+        for half in range(2):
+            tokens = mixed[group, half, pl.ds(0, GCAP), :]
+            low = low + lax.dot_general(
+                mixed[group, half, pl.ds(GCAP, 16), :], tokens, (((1,), (1,)), ((), ())),
+                preferred_element_type=F32,
+            )
+            part = part + jnp.dot(
+                tokens, out_w[half * half_rows : (half + 1) * half_rows, :],
+                preferred_element_type=F32,
+            )
+
+        @pl.when(group != r)
+        def _():
+            lowo_out[group] = low
+            lowo_copy(group).start()
+            res_out[group] = part.astype(BF)
+            res_copy(group).start()
+
+        @pl.when(group == r)
+        def _():
+            lowo_own[...] = low
+            res_own[...] = part
+
+    def second(step, _):
+        side = step % 2
+        group = r + (step // 2) * (2 * side - 1)
+
+        @pl.when((group >= 0) & (group < planes) & (step != 1))
+        def _():
+            combine(group)
+
+        return 0
+
+    lax.fori_loop(0, 2 * planes, second, 0)
+
+    _, request, _ = layout(r, 0)
+    alive = jnp.where(request != -2, 1.0, 0.0)
+    low = lowo_own[...]
+    total = res_own[...] + out_bias[...].astype(F32)
+    for step in range(1, rows):
+        peer = (r + step) % rows
+        to(
+            lowo_out.at[peer], lowo_in.at[peer], lowo_send.at[peer], lowo_recv.at[peer], r, c
+        ).wait_recv()
+        low = low + lowo_in[peer]
+    for step in range(1, rows):
+        peer = (r + step) % rows
+        to(
+            res_out.at[peer], res_in.at[peer], res_send.at[peer], res_recv.at[peer], r, c
+        ).wait_recv()
+        total = total + res_in[peer].astype(F32)
+    total = total + lax.dot_general(
+        low.astype(BF), up_out[adapter(r)], (((0,), (0,)), ((), ())), preferred_element_type=F32
+    )
+    out[...] = (total * alive).astype(BF)
+
+    for step in range(1, rows):
+        peer = (r + step) % rows
+        stat_copy(peer).wait_send()
+        res_copy(peer).wait_send()
+        lowo_copy(peer).wait_send()
+
+    def drain(group, _):
+        @pl.when((group <= z) & (z < planes - 1))
+        def _():
+            x_copy(0, group, c + 2).wait_send()
+
+        @pl.when((group >= z) & (z > 0))
+        def _():
+            x_copy(1, group, c - 2).wait_send()
+
+        x_copy(2, group, sib).wait_send()
+        for step in range(1, rows):
+            peer = (r + step) % rows
+            low_copy(group, peer).wait_send()
+            part_copy(group, peer).wait_send()
+
+        @pl.when(r != z)
+        def _():
+            mixed_copy(group, r).wait_send()
+
+        @pl.when((z >= r) & (z < planes - 1))
+        def _():
+            chain_copy(0, group, c + 2).wait_send()
+
+        @pl.when((z <= r) & (z > 0))
+        def _():
+            chain_copy(1, group, c - 2).wait_send()
+
+        chain_copy(2, group, sib).wait_send()
+        return 0
+
+    lax.fori_loop(0, planes, drain, 0)
+
+
+def fused(
+    hidden,
+    ln_gain,
+    ln_shift,
+    qkv_weight,
+    qkv_bias,
+    out_weight,
+    out_bias,
+    down_qkv,
+    up_qkv,
+    down_out,
+    up_out,
+    prompt_lens,
+    suffix_lens,
+    group_sizes,
+    group_adapter_choice,
+    chosen,
+):
+    groups = lax.axis_size("row")
+    block, width = hidden.shape
+    out_cols = out_weight.shape[1]
+    bank, rank = down_out.shape[0], down_out.shape[1]
+    down_t = jnp.transpose(down_qkv, (0, 2, 1))
+    vmem = pl.BlockSpec(memory_space=pltpu.VMEM)
+    smem = pl.BlockSpec(memory_space=pltpu.SMEM)
+    hbm = pl.BlockSpec(memory_space=pl.ANY)
+    dma = pltpu.SemaphoreType.DMA
+    half = HEAD_SIZE * groups
+    macs = groups * GCAP * (qkv_weight.size + out_weight.size)
+    return pl.pallas_call(
+        functools.partial(fused_kernel, groups),
+        out_shape=jax.ShapeDtypeStruct((GCAP, out_cols), BF),
+        in_specs=[vmem] * 5 + [smem] * 5 + [hbm] * 6,
+        out_specs=vmem,
+        scratch_shapes=[
+            pltpu.VMEM(qkv_weight.shape, BF),
+            pltpu.VMEM(out_weight.shape, BF),
+            pltpu.VMEM(down_t.shape, BF),
+            pltpu.VMEM((bank, rank, HIDDEN_PART), BF),
+            pltpu.VMEM(down_out.shape, BF),
+            pltpu.VMEM(up_out.shape, BF),
+            pltpu.VMEM((groups, block, 128), F32),
+            pltpu.VMEM((groups * GCAP, width), BF),
+            pltpu.VMEM((groups, groups, GCAP, HIDDEN_PART), BF),
+            pltpu.VMEM((groups, groups, GCAP, HIDDEN_PART), BF),
+            pltpu.VMEM((groups, GCAP, HIDDEN_PART), F32),
+            pltpu.VMEM((groups, rank, GCAP), F32),
+            pltpu.VMEM((groups, groups, rank, GCAP), F32),
+            pltpu.VMEM((groups, GCAP, HEAD_SIZE), BF),
+            pltpu.VMEM((groups, 2, GCAP + rank, half), BF),
+            pltpu.VMEM((groups, GCAP, out_cols), BF),
+            pltpu.VMEM((groups, GCAP, out_cols), BF),
+            pltpu.VMEM((GCAP, out_cols), F32),
+            pltpu.VMEM((groups, rank, GCAP), F32),
+            pltpu.VMEM((groups, rank, GCAP), F32),
+            pltpu.VMEM((rank, GCAP), F32),
+            dma((6,)),
+            dma((groups,)),
+            dma((groups,)),
+            dma((3, groups)),
+            dma((2 * groups,)),
+            dma((groups, groups)),
+            dma((groups, groups)),
+            dma((groups, groups)),
+            dma((groups, groups)),
+            dma((groups,)),
+            dma((groups, groups)),
+            dma((3, groups)),
+            dma((groups, 2)),
+            dma((groups,)),
+            dma((groups,)),
+            dma((groups,)),
+            dma((groups,)),
+        ],
+        compiler_params=pltpu.CompilerParams(
+            collective_id=0, has_side_effects=True, vmem_limit_bytes=52 * 2**20
+        ),
+        cost_estimate=pl.CostEstimate(
+            flops=2 * macs, bytes_accessed=2 * (qkv_weight.size + out_weight.size), transcendentals=0
+        ),
+    )(
+        hidden,
+        ln_gain[None],
+        ln_shift[None],
+        qkv_bias[None],
+        out_bias[None],
+        prompt_lens,
+        suffix_lens,
+        group_sizes,
+        group_adapter_choice,
+        chosen,
+        qkv_weight,
+        out_weight,
+        down_t,
+        up_qkv,
+        down_out,
+        up_out,
+    )
+
+
+def block_of(*arrays):
+    groups = lax.axis_size("row")
+    heads_here = arrays[4].shape[0] // HIDDEN_PART
+    if heads_here == groups and lax.axis_size("col") == 2 * groups and arrays[5].shape[1] % 128 == 0:
+        return fused(*arrays)
+    return local(*arrays)
+
+
 def solution(mesh):
     in_specs = (
         P("col", "row"),
@@ -149,4 +764,4 @@
         P(),
     )
     out_specs = P("row", "col")
-    return jax.shard_map(local, mesh=mesh, in_specs=in_specs, out_specs=out_specs, check_vma=False)
+    return jax.shard_map(block_of, mesh=mesh, in_specs=in_specs, out_specs=out_specs, check_vma=False)

time: 189 us -> 93.1 us (0.49)
  Pallas kernels: 0 us -> 83.5 us
  waiting for transfers between devices: 65 us -> 0 us
  blocking collectives: 44.4 us -> 0 us
  matrix products: 21.9 us -> 0 us
  other arithmetic: 17.9 us -> 0 us
  between operations: 15.5 us -> 0.02 us
  starting transfers between devices: 12.7 us -> 0 us
    pallas_call x0 -> x1, Pallas kernels: none -> 83.5 us  [fused(): pl.pallas_call(functools.partial(fused_kernel, groups), out_shape=jax.Sha...]
    all_gather x2 -> x0, waiting for transfers between devices: 49.4 us -> none  [the longest x1 27.2 us: local(): tokens = lax.all_gather(normed, 'col', axis=0, tiled=True)]
    all_gather x2 -> x0, blocking collectives: 23.5 us -> none  [the longest x1 13.9 us: local(): down_full = lax.all_gather(down_out[own_adapter], 'col', axis=1, tiled=True)]
    all_to_all x1 -> x0, blocking collectives: 20.9 us -> none  [local(): lax.all_to_all(all_heads, 'row', split_axis=1, concat_axis=0, tiled=True)]
    dot_general x6 -> x0, matrix products: 19.6 us -> none  [the longest x1 8.24 us: local(): jnp.dot(tokens, qkv_weight, preferred_element_type=jnp.float32)]
    all_to_all x3 -> x0, waiting for transfers between devices: 15.6 us -> none  [sum_over_row(): lax.all_to_all(partial, 'row', split_axis=0, concat_axis=0, tiled=True)]
    all_to_all x3 -> x0, starting transfers between devices: 12.6 us -> none  [sum_over_row(): lax.all_to_all(partial, 'row', split_axis=0, concat_axis=0, tiled=True)]
    reduce_sum x9 -> x0, other arithmetic: 6.94 us -> none  [the longest x3 4.25 us: sum_over_row(): return jnp.sum(blocks.astype(jnp.float32), axis=0)]
  transfers between devices with their start and end apart: 5 -> 0, of which waited for: 3 -> 0; matrix products, arithmetic and copies ran while one was open for 10% -> 0% of each run, Pallas kernels for 0% -> 0%
where the time goes in v2:
time: 93.1 us; the launch traced here: 92.5 us
  Pallas kernels  83.5 us (90%)
  local copies, waits for them, and re-layouts  8.96 us (10%)
    pallas_call x1, Pallas kernels, fused(): pl.pallas_call(functools.partial(fused_kernel, groups), out_shape=jax.Sha...  83.5 us
    unnamed x15, local copies, waits for them, and re-layouts  6.2 us

profile of v2, /device:TPU:0, one launch (start us, length us, event | category | flops | bytes accessed | tf_op | source)
XLA Modules:
  0.0 92.5 jit_solution(12326024974977823351)
XLA Ops:
  0.0 0.7 broadcast_in_dim.15.out_bias
  0.7 0.7 broadcast_in_dim.14.qkv_bias
  1.4 0.7 broadcast_in_dim.12.gain
  2.1 0.7 broadcast_in_dim.13.shift
  2.8 0.0 copy-start
  2.8 1.2 %copy-done = bf16[64,16,512]{2,1,0:T(8,128)(2,1)S(1)} copy-done((bf16[64,16,512]{2,1,0:T(8,128)(2,1)S(1)}, bf16[64,16,512]{2,1,0:T(8,128)(2,1)}, u32[]{:S(2)}) %copy-start) | copy-done | bytes 1048600
  4.0 0.0 copy-start.1
  4.0 1.0 %copy-done.1 = bf16[80,1792]{1,0:T(8,128)(2,1)S(1)} copy-done((bf16[80,1792]{1,0:T(8,128)(2,1)S(1)}, bf16[80,1792]{1,0:T(8,128)(2,1)}, u32[]{:S(2)}) %copy-start.1) | copy-done | bytes 286744
  4.9 0.0 copy-start.2
  5.0 0.7 copy-done.2
  5.6 0.0 copy-start.3
  5.6 0.7 copy-done.3
  6.3 0.0 copy-start.4
  6.3 0.7 copy-done.4
  6.9 0.0 copy-start.5
  6.9 0.7 copy-done.5
  7.6 0.0 copy-start.6
  7.6 0.7 copy-done.6
  8.3 83.5 %shard_map.154 = bf16[160,896]{1,0:T(8,128)(2,1)S(1)} custom-call(bf16[80,1792]{1,0:T(8,128)(2,1)S(1)} %copy-done.1, bf16[1,1792]{1,0:T(2,128)(2,1)S(1)} %broadcast_in_dim.12.gain, bf16[1,1792]{1,0:T(2,128)(2,1)S(1)} %broadcast_in_dim.13.shift, bf16[1,1536]{1,0:T(2,128)(2,1)S(1)} %broadcast_in_dim.14.qkv_bias, bf16[1,896]{1,0:T(2,128)(2,1)S(1)} %broadcast_in_dim.15.out_bias, ...), custom_call_target="tpu_custom_call" | custom-call | flops 4697620480 | bytes 7340032 | tf_op jit(solution)/shard_map/pallas_call | solution.py:668
  91.7 0.7 copy.18
Async XLA Ops:
  2.8 1.2 %copy-start = (bf16[64,16,512]{2,1,0:T(8,128)(2,1)S(1)}, bf16[64,16,512]{2,1,0:T(8,128)(2,1)}, u32[]{:S(2)}) copy-start(bf16[64,16,512]{2,1,0:T(8,128)(2,1)} %down_out_hbm.1) | copy-start | bytes 3145732
  4.0 1.0 %copy-start.1 = (bf16[80,1792]{1,0:T(8,128)(2,1)S(1)}, bf16[80,1792]{1,0:T(8,128)(2,1)}, u32[]{:S(2)}) copy-start(bf16[80,1792]{1,0:T(8,128)(2,1)} %hidden.1) | copy-start | bytes 860164
  4.9 0.7 copy-start.2
  5.6 0.7 copy-start.3
  6.3 0.7 copy-start.4
  6.9 0.7 copy-start.5
  7.6 0.7 copy-start.6

commit v3 on v2

--- a/solution.py
+++ b/solution.py
@@ -140,6 +140,23 @@
 
 def fused_kernel(
     planes,
+    hidden_hbm,
+    gain_hbm,
+    shift_hbm,
+    qkv_bias_hbm,
+    out_bias_hbm,
+    prompt_lens_hbm,
+    suffix_lens_hbm,
+    group_sizes_hbm,
+    choice_hbm,
+    chosen_hbm,
+    qkv_hbm,
+    out_hbm,
+    down_qkv_hbm,
+    up_qkv_hbm,
+    down_out_hbm,
+    up_out_hbm,
+    out,
     hidden,
     gain,
     shift,
@@ -150,13 +167,6 @@
     group_sizes,
     choice,
     chosen,
-    qkv_hbm,
-    out_hbm,
-    down_qkv_hbm,
-    up_qkv_hbm,
-    down_out_hbm,
-    up_out_hbm,
-    out,
     qkv_w,
     out_w,
     down_qkv,
@@ -178,6 +188,7 @@
     lowo_out,
     lowo_in,
     lowo_own,
+    own_bias,
     load_sem,
     stat_send,
     stat_recv,
@@ -224,8 +235,18 @@
         pltpu.make_async_copy(down_out_hbm, down_out, load_sem.at[3]),
         pltpu.make_async_copy(out_hbm, out_w, load_sem.at[4]),
         pltpu.make_async_copy(up_out_hbm, up_out, load_sem.at[5]),
+        pltpu.make_async_copy(hidden_hbm, hidden, load_sem.at[6]),
+        pltpu.make_async_copy(gain_hbm, gain, load_sem.at[7]),
+        pltpu.make_async_copy(shift_hbm, shift, load_sem.at[8]),
+        pltpu.make_async_copy(qkv_bias_hbm, qkv_bias, load_sem.at[9]),
+        pltpu.make_async_copy(out_bias_hbm, out_bias, load_sem.at[10]),
+        pltpu.make_async_copy(prompt_lens_hbm, prompt_lens, load_sem.at[11]),
+        pltpu.make_async_copy(suffix_lens_hbm, suffix_lens, load_sem.at[12]),
+        pltpu.make_async_copy(group_sizes_hbm, group_sizes, load_sem.at[13]),
+        pltpu.make_async_copy(choice_hbm, choice, load_sem.at[14]),
+        pltpu.make_async_copy(chosen_hbm, chosen, load_sem.at[15]),
     ]
-    for load in loads:
+    for load in loads[6:] + loads[:6]:
         load.start()
 
     barrier = pltpu.get_barrier_semaphore()
@@ -251,6 +272,7 @@
     after = (2 * planes - 2 - z) // planes
     pl.semaphore_wait(barrier, rows + before + after)
 
+    loads[6].wait()
     wide = hidden[...].astype(F32)
     width = wide.shape[1]
     own_mean = jnp.mean(wide, axis=1, keepdims=True)
@@ -273,14 +295,17 @@
     spread = spread + width * sum((m - average) * (m - average) for m in means)
     spread = spread / (width * rows)
 
+    loads[7].wait()
+    loads[8].wait()
+
     def x_rows(index):
         return pl.ds(pl.multiple_of(index * block, 16), block)
 
     x[x_rows(c), :] = (
         (hidden[...].astype(F32) - average)
         * lax.rsqrt(spread + 1e-05)
-        * gain[...].astype(F32)
-        + shift[...].astype(F32)
+        * gain[...].astype(F32)[None]
+        + shift[...].astype(F32)[None]
     ).astype(BF)
 
     def x_copy(way, group, col):
@@ -394,7 +419,7 @@
 
     def attend(group):
         low = low_own[group]
-        proj = part_own[group] + qkv_bias[:, pl.ds(head_col, HIDDEN_PART)].astype(F32)
+        proj = part_own[group] + own_bias[...]
         for step in range(1, rows):
             peer = (r + step) % rows
             to(
@@ -436,66 +461,8 @@
             mixed_out[group] = rows_mixed
             mixed_copy(group, r).start()
 
-    loads[0].wait()
-    loads[1].wait()
-    loads[2].wait()
-    loads[3].wait()
-
-    def first(step, _):
-        @pl.when(step < planes)
-        def _():
-            for side in range(2):
-                group = z + step * (2 * side - 1)
-                valid = (group >= 0) & (group < planes)
-                if side == 1:
-                    valid = valid & (step > 0)
-
-                @pl.when(valid)
-                def _():
-                    @pl.when(step > 0)
-                    def _():
-                        x_wait(2 * group + k)
-
-                    @pl.when((group <= z) & (z < planes - 1))
-                    def _():
-                        x_copy(0, group, c + 2).start()
-
-                    @pl.when((group >= z) & (z > 0))
-                    def _():
-                        x_copy(1, group, c - 2).start()
-
-                    x_copy(2, group, sib).start()
-
-            def compute(side, _):
-                group = z + step * (2 * side - 1)
-
-                @pl.when((group >= 0) & (group < planes) & (step + 1 - side > 0))
-                def _():
-                    x_wait(2 * group + 1 - k)
-                    project(group)
-
-                return 0
-
-            lax.fori_loop(0, 2, compute, 0)
-
-        @pl.when(step > 0)
-        def _():
-            def mix(side, _):
-                group = z + (step - 1) * (2 * side - 1)
-
-                @pl.when((group >= 0) & (group < planes) & (step - side > 0))
-                def _():
-                    attend(group)
-
-                return 0
-
-            lax.fori_loop(0, 2, mix, 0)
-
-        return 0
-
-    lax.fori_loop(0, planes + 1, first, 0)
-    loads[4].wait()
-    loads[5].wait()
+    for load in loads[:6] + loads[9:]:
+        load.wait()
 
     def chain_copy(way, group, col):
         return to(
@@ -564,22 +531,85 @@
             lowo_own[...] = low
             res_own[...] = part
 
-    def second(step, _):
-        side = step % 2
-        group = r + (step // 2) * (2 * side - 1)
-
-        @pl.when((group >= 0) & (group < planes) & (step != 1))
-        def _():
-            combine(group)
+    bias = qkv_bias[...].astype(F32)[None]
+    own_bias[...] = sum(
+        jnp.where(r == head, bias[:, head * HIDDEN_PART : (head + 1) * HIDDEN_PART], 0.0)
+        for head in range(rows)
+    )
+
+    def first(step, _):
+        @pl.when(step < planes)
+        def _():
+            for side in range(2):
+                group = z + step * (2 * side - 1)
+                valid = (group >= 0) & (group < planes)
+                if side == 1:
+                    valid = valid & (step > 0)
+
+                @pl.when(valid)
+                def _():
+                    @pl.when(step > 0)
+                    def _():
+                        x_wait(2 * group + k)
+
+                    @pl.when((group <= z) & (z < planes - 1))
+                    def _():
+                        x_copy(0, group, c + 2).start()
+
+                    @pl.when((group >= z) & (z > 0))
+                    def _():
+                        x_copy(1, group, c - 2).start()
+
+                    x_copy(2, group, sib).start()
+
+            def compute(side, _):
+                group = z + step * (2 * side - 1)
+
+                @pl.when((group >= 0) & (group < planes) & (step + 1 - side > 0))
+                def _():
+                    x_wait(2 * group + 1 - k)
+                    project(group)
+
+                return 0
+
+            lax.fori_loop(0, 2, compute, 0)
+
+        @pl.when((step > 0) & (step <= planes))
+        def _():
+            def mix(side, _):
+                group = z + (step - 1) * (2 * side - 1)
+
+                @pl.when((group >= 0) & (group < planes) & (step - side > 0))
+                def _():
+                    attend(group)
+
+                return 0
+
+            lax.fori_loop(0, 2, mix, 0)
+
+        behind = step - 2 - ((r - z) * (r - z) + planes * planes - 1) // (planes * planes)
+
+        @pl.when((behind >= 0) & (behind < planes))
+        def _():
+            def join(side, _):
+                group = r + behind * (2 * side - 1)
+
+                @pl.when((group >= 0) & (group < planes) & (behind + 1 - side > 0))
+                def _():
+                    combine(group)
+
+                return 0
+
+            lax.fori_loop(0, 2, join, 0)
 
         return 0
 
-    lax.fori_loop(0, 2 * planes, second, 0)
+    lax.fori_loop(0, planes + 3, first, 0)
 
     _, request, _ = layout(r, 0)
     alive = jnp.where(request != -2, 1.0, 0.0)
     low = lowo_own[...]
-    total = res_own[...] + out_bias[...].astype(F32)
+    total = res_own[...] + out_bias[...].astype(F32)[None]
     for step in range(1, rows):
         peer = (r + step) % rows
         to(
@@ -660,7 +690,6 @@
     bank, rank = down_out.shape[0], down_out.shape[1]
     down_t = jnp.transpose(down_qkv, (0, 2, 1))
     vmem = pl.BlockSpec(memory_space=pltpu.VMEM)
-    smem = pl.BlockSpec(memory_space=pltpu.SMEM)
     hbm = pl.BlockSpec(memory_space=pl.ANY)
     dma = pltpu.SemaphoreType.DMA
     half = HEAD_SIZE * groups
@@ -668,9 +697,19 @@
     return pl.pallas_call(
         functools.partial(fused_kernel, groups),
         out_shape=jax.ShapeDtypeStruct((GCAP, out_cols), BF),
-        in_specs=[vmem] * 5 + [smem] * 5 + [hbm] * 6,
+        in_specs=[hbm] * 16,
         out_specs=vmem,
         scratch_shapes=[
+            pltpu.VMEM(hidden.shape, BF),
+            pltpu.VMEM(ln_gain.shape, BF),
+            pltpu.VMEM(ln_shift.shape, BF),
+            pltpu.VMEM(qkv_bias.shape, BF),
+            pltpu.VMEM(out_bias.shape, BF),
+            pltpu.SMEM(prompt_lens.shape, jnp.int32),
+            pltpu.SMEM(suffix_lens.shape, jnp.int32),
+            pltpu.SMEM(group_sizes.shape, jnp.int32),
+            pltpu.SMEM(group_adapter_choice.shape, jnp.int32),
+            pltpu.SMEM(chosen.shape, jnp.int32),
             pltpu.VMEM(qkv_weight.shape, BF),
             pltpu.VMEM(out_weight.shape, BF),
             pltpu.VMEM(down_t.shape, BF),
@@ -692,7 +731,8 @@
             pltpu.VMEM((groups, rank, GCAP), F32),
             pltpu.VMEM((groups, rank, GCAP), F32),
             pltpu.VMEM((rank, GCAP), F32),
-            dma((6,)),
+            pltpu.VMEM((1, HIDDEN_PART), F32),
+            dma((16,)),
             dma((groups,)),
             dma((groups,)),
             dma((3, groups)),
@@ -711,17 +751,17 @@
             dma((groups,)),
         ],
         compiler_params=pltpu.CompilerParams(
-            collective_id=0, has_side_effects=True, vmem_limit_bytes=52 * 2**20
+            collective_id=0, has_side_effects=True, vmem_limit_bytes=60 * 2**20
         ),
         cost_estimate=pl.CostEstimate(
             flops=2 * macs, bytes_accessed=2 * (qkv_weight.size + out_weight.size), transcendentals=0
         ),
     )(
         hidden,
-        ln_gain[None],
-        ln_shift[None],
-        qkv_bias[None],
-        out_bias[None],
+        ln_gain,
+        ln_shift,
+        qkv_bias,
+        out_bias,
         prompt_lens,
         suffix_lens,
         group_sizes,

time: 93.1 us -> 85.6 us (0.919)
  local copies, waits for them, and re-layouts: 8.96 us -> 1.69 us
    unnamed x15 -> x1, local copies, waits for them, and re-layouts: 6.2 us -> 1.69 us
    broadcast_in_dim x4 -> x0, local copies, waits for them, and re-layouts: 2.76 us -> none  [the longest x1 0.69 us: fused(): ln_gain[None]]
where the time goes in v3:
time: 85.6 us; the launch traced here: 85.4 us
  Pallas kernels  83.7 us (98%)
  local copies, waits for them, and re-layouts  1.69 us (2%)
    pallas_call x1, Pallas kernels, fused(): pl.pallas_call(functools.partial(fused_kernel, groups), out_shape=jax.Sha...  83.7 us

profile of v3, /device:TPU:0, one launch (start us, length us, event | category | flops | bytes accessed | tf_op | source)
XLA Modules:
  0.0 85.4 jit_solution(2575104705958997940)
XLA Ops:
  0.0 83.7 %shard_map.154 = bf16[160,896]{1,0:T(8,128)(2,1)} custom-call(bf16[80,1792]{1,0:T(8,128)(2,1)} %hidden_hbm.1, bf16[1792]{0:T(1024)(128)(2,1)} %gain_hbm.1, bf16[1792]{0:T(1024)(128)(2,1)} %shift_hbm.1, bf16[1536]{0:T(1024)(128)(2,1)} %qkv_bias_hbm.1, bf16[896]{0:T(1024)(128)(2,1)} %out_bias_hbm.1, s32[4]{0:T(128)} %prompt_lens_hbm.1, ...), custom_call_target="tpu_custom_call" | custom-call | flops 4697620480 | bytes 7340032 | tf_op jit(solution)/shard_map/pallas_call | solution.py:697
  83.7 1.7 %copy.18 = bf16[160,896]{1,0:T(8,128)(2,1)} copy(bf16[160,896]{1,0:T(8,128)(2,1)} %shard_map.154) | data formatting | bytes 573440

commit v4 on v3

--- a/solution.py
+++ b/solution.py
@@ -461,19 +461,25 @@
             mixed_out[group] = rows_mixed
             mixed_copy(group, r).start()
 
-    for load in loads[:6] + loads[9:]:
+    for load in loads[9:]:
         load.wait()
 
-    def chain_copy(way, group, col):
+    parts = chain_recv.shape[2]
+    part_width = mixed.shape[3] // parts
+
+    def chain_at(group, half, part):
+        return mixed.at[group, half, :, pl.ds(part * part_width, part_width)]
+
+    def chain_copy(way, group, part, col):
         return to(
-            mixed.at[group, k], mixed.at[group, k],
-            chain_send.at[way, group], chain_recv.at[group, k], r, col,
-        )
-
-    def chain_wait(group, half):
+            chain_at(group, k, part), chain_at(group, k, part),
+            chain_send.at[way, group, part], chain_recv.at[group, k, part], r, col,
+        )
+
+    def chain_wait(group, half, part):
         to(
-            mixed.at[group, half], mixed.at[group, half],
-            chain_send.at[0, group], chain_recv.at[group, half], r, c,
+            chain_at(group, half, part), chain_at(group, half, part),
+            chain_send.at[0, group, part], chain_recv.at[group, half, part], r, c,
         ).wait_recv()
 
     def res_copy(group):
@@ -492,20 +498,22 @@
             for step in range(1, rows):
                 mixed_copy(group, (r + step) % rows).wait_recv()
 
-        @pl.when(z != r)
-        def _():
-            chain_wait(group, k)
-
-        @pl.when((z >= r) & (z < planes - 1))
-        def _():
-            chain_copy(0, group, c + 2).start()
-
-        @pl.when((z <= r) & (z > 0))
-        def _():
-            chain_copy(1, group, c - 2).start()
-
-        chain_copy(2, group, sib).start()
-        chain_wait(group, 1 - k)
+        for part in range(parts):
+            @pl.when(z != r)
+            def _():
+                chain_wait(group, k, part)
+
+            @pl.when((z >= r) & (z < planes - 1))
+            def _():
+                chain_copy(0, group, part, c + 2).start()
+
+            @pl.when((z <= r) & (z > 0))
+            def _():
+                chain_copy(1, group, part, c - 2).start()
+
+            chain_copy(2, group, part, sib).start()
+        for part in range(parts):
+            chain_wait(group, 1 - k, part)
         low = jnp.zeros((16, GCAP), F32)
         part = jnp.zeros((GCAP, out_w.shape[1]), F32)
         for half in range(2):
@@ -562,6 +570,11 @@
 
                     x_copy(2, group, sib).start()
 
+            @pl.when(step == 0)
+            def _():
+                for load in loads[:6]:
+                    load.wait()
+
             def compute(side, _):
                 group = z + step * (2 * side - 1)
 
@@ -574,6 +587,21 @@
 
             lax.fori_loop(0, 2, compute, 0)
 
+        behind = step - 2 - ((r - z) * (r - z) + planes * planes - 1) // (planes * planes)
+
+        @pl.when((behind >= 0) & (behind < planes))
+        def _():
+            def join(side, _):
+                group = r + behind * (2 * side - 1)
+
+                @pl.when((group >= 0) & (group < planes) & (behind + 1 - side > 0))
+                def _():
+                    combine(group)
+
+                return 0
+
+            lax.fori_loop(0, 2, join, 0)
+
         @pl.when((step > 0) & (step <= planes))
         def _():
             def mix(side, _):
@@ -586,21 +614,6 @@
                 return 0
 
             lax.fori_loop(0, 2, mix, 0)
-
-        behind = step - 2 - ((r - z) * (r - z) + planes * planes - 1) // (planes * planes)
-
-        @pl.when((behind >= 0) & (behind < planes))
-        def _():
-            def join(side, _):
-                group = r + behind * (2 * side - 1)
-
-                @pl.when((group >= 0) & (group < planes) & (behind + 1 - side > 0))
-                def _():
-                    combine(group)
-
-                return 0
-
-            lax.fori_loop(0, 2, join, 0)
 
         return 0
 
@@ -652,15 +665,16 @@
         def _():
             mixed_copy(group, r).wait_send()
 
-        @pl.when((z >= r) & (z < planes - 1))
-        def _():
-            chain_copy(0, group, c + 2).wait_send()
-
-        @pl.when((z <= r) & (z > 0))
-        def _():
-            chain_copy(1, group, c - 2).wait_send()
-
-        chain_copy(2, group, sib).wait_send()
+        for part in range(parts):
+            @pl.when((z >= r) & (z < planes - 1))
+            def _():
+                chain_copy(0, group, part, c + 2).wait_send()
+
+            @pl.when((z <= r) & (z > 0))
+            def _():
+                chain_copy(1, group, part, c - 2).wait_send()
+
+            chain_copy(2, group, part, sib).wait_send()
         return 0
 
     lax.fori_loop(0, planes, drain, 0)
@@ -743,8 +757,8 @@
             dma((groups, groups)),
             dma((groups,)),
             dma((groups, groups)),
-            dma((3, groups)),
-            dma((groups, 2)),
+            dma((3, groups, 2)),
+            dma((groups, 2, 2)),
             dma((groups,)),
             dma((groups,)),
             dma((groups,)),

time: 85.6 us -> 94 us (1.098)
  Pallas kernels: 83.7 us -> 92.2 us
    pallas_call x1, Pallas kernels: 83.7 us -> 92.2 us  [fused(): pl.pallas_call(functools.partial(fused_kernel, groups), out_shape=jax.Sha...]
where the time goes in v4:
time: 94 us; the launch traced here: 93.9 us
  Pallas kernels  92.2 us (98%)
  local copies, waits for them, and re-layouts  1.69 us (2%)
    pallas_call x1, Pallas kernels, fused(): pl.pallas_call(functools.partial(fused_kernel, groups), out_shape=jax.Sha...  92.2 us

profile of v4, /device:TPU:0, one launch (start us, length us, event | category | flops | bytes accessed | tf_op | source)
XLA Modules:
  0.0 93.9 jit_solution(16307522935120552567)
XLA Ops:
  0.0 92.2 %shard_map.154 = bf16[160,896]{1,0:T(8,128)(2,1)} custom-call(bf16[80,1792]{1,0:T(8,128)(2,1)} %hidden_hbm.1, bf16[1792]{0:T(1024)(128)(2,1)} %gain_hbm.1, bf16[1792]{0:T(1024)(128)(2,1)} %shift_hbm.1, bf16[1536]{0:T(1024)(128)(2,1)} %qkv_bias_hbm.1, bf16[896]{0:T(1024)(128)(2,1)} %out_bias_hbm.1, s32[4]{0:T(128)} %prompt_lens_hbm.1, ...), custom_call_target="tpu_custom_call" | custom-call | flops 4697620480 | bytes 7340032 | tf_op jit(solution)/shard_map/pallas_call | solution.py:711
  92.2 1.7 %copy.18 = bf16[160,896]{1,0:T(8,128)(2,1)} copy(bf16[160,896]{1,0:T(8,128)(2,1)} %shard_map.154) | data formatting | bytes 573440

commit v5 on v4

--- a/solution.py
+++ b/solution.py
@@ -572,8 +572,8 @@
 
             @pl.when(step == 0)
             def _():
-                for load in loads[:6]:
-                    load.wait()
+                loads[0].wait()
+                loads[1].wait()
 
             def compute(side, _):
                 group = z + step * (2 * side - 1)
@@ -587,7 +587,26 @@
 
             lax.fori_loop(0, 2, compute, 0)
 
-        behind = step - 2 - ((r - z) * (r - z) + planes * planes - 1) // (planes * planes)
+        @pl.when((step > 0) & (step <= planes))
+        def _():
+            @pl.when(step == 1)
+            def _():
+                for load in loads[2:6]:
+                    load.wait()
+
+            def mix(side, _):
+                group = z + (step - 1) * (2 * side - 1)
+
+                @pl.when((group >= 0) & (group < planes) & (step - side > 0))
+                def _():
+                    attend(group)
+
+                return 0
+
+            lax.fori_loop(0, 2, mix, 0)
+
+        away = ((r - z) * (r - z) + planes * planes - 1) // (planes * planes)
+        behind = step - 2 - away * (planes - 1)
 
         @pl.when((behind >= 0) & (behind < planes))
         def _():
@@ -602,22 +621,9 @@
 
             lax.fori_loop(0, 2, join, 0)
 
-        @pl.when((step > 0) & (step <= planes))
-        def _():
-            def mix(side, _):
-                group = z + (step - 1) * (2 * side - 1)
-
-                @pl.when((group >= 0) & (group < planes) & (step - side > 0))
-                def _():
-                    attend(group)
-
-                return 0
-
-            lax.fori_loop(0, 2, mix, 0)
-
         return 0
 
-    lax.fori_loop(0, planes + 3, first, 0)
+    lax.fori_loop(0, 2 * planes + 1, first, 0)
 
     _, request, _ = layout(r, 0)
     alive = jnp.where(request != -2, 1.0, 0.0)

time: 94 us -> 81.6 us (0.87)
  Pallas kernels: 92.2 us -> 79.8 us
    pallas_call x1, Pallas kernels: 92.2 us -> 79.8 us  [fused(): pl.pallas_call(functools.partial(fused_kernel, groups), out_shape=jax.Sha...]
where the time goes in v5:
time: 81.6 us; the launch traced here: 81.5 us
  Pallas kernels  79.8 us (98%)
  local copies, waits for them, and re-layouts  1.69 us (2%)
    pallas_call x1, Pallas kernels, fused(): pl.pallas_call(functools.partial(fused_kernel, groups), out_shape=jax.Sha...  79.8 us
    unnamed x1, local copies, waits for them, and re-layouts  1.69 us

profile of v5, /device:TPU:0, one launch (start us, length us, event | category | flops | bytes accessed | tf_op | source)
XLA Modules:
  0.0 81.5 jit_solution(18371719336799551114)
XLA Ops:
  0.0 79.8 %shard_map.154 = bf16[160,896]{1,0:T(8,128)(2,1)} custom-call(bf16[80,1792]{1,0:T(8,128)(2,1)} %hidden_hbm.1, bf16[1792]{0:T(1024)(128)(2,1)} %gain_hbm.1, bf16[1792]{0:T(1024)(128)(2,1)} %shift_hbm.1, bf16[1536]{0:T(1024)(128)(2,1)} %qkv_bias_hbm.1, bf16[896]{0:T(1024)(128)(2,1)} %out_bias_hbm.1, s32[4]{0:T(128)} %prompt_lens_hbm.1, ...), custom_call_target="tpu_custom_call" | custom-call | flops 4697620480 | bytes 7340032 | tf_op jit(solution)/shard_map/pallas_call | solution.py:717
  79.8 1.7 %copy.18 = bf16[160,896]{1,0:T(8,128)(2,1)} copy(bf16[160,896]{1,0:T(8,128)(2,1)} %shard_map.154) | data formatting | bytes 573440
